TPU v7x, 512 devices: a whole 4x8x8 slice. The times are simulated.
512 devices in a mesh: blk: 64 (over y, z_hi, core), head: 8 (over z_lo, x).
Axes of the slice: x: 4, y: 8, z: 8 (z_hi: 4, z_lo: 2; z = z_hi * 2 + z_lo), core: 2. Of those that a mesh axis runs over, the one named last changes fastest.
Arguments:
- query_nope: bfloat16 [4096, 8192], P('blk', 'head'), may hold values from -140 to 140
- query_rope: bfloat16 [4096, 4096], P('blk', 'head'), may hold values from -6 to 6
- compressed: bfloat16 [4096, 576], P(('blk', 'head')), may hold values from -6 to 6
- latent_gain: float32 [512], replicated, may hold values from 0.1 to 1.9
- key_up: bfloat16 [64, 128, 512], P('head'), may hold values from -0.5 to 0.5
- value_up: bfloat16 [64, 512, 128], P('head'), may hold values from -1.5 to 1.5
- span_order: int32 [128], replicated, may hold values from 0 to 127, each once
Outputs:
- attended: bfloat16 [4096, 8192], P('blk', 'head')
Inputs may be any that keep to these rules, and one draw needn't show every extreme that they name: Every number appears once; device index i of blk holds the blocks span_order[2 i] and span_order[2 i + 1].
All inputs are finite; a program needn't handle non-finite values.
Results may differ from a plain program's by a relative error of at most 0.0075.
The roundings to bfloat16 on the way count: a program that leaves them out, or rounds other values in their place, can miss the bound.
Values may be sent and summed in bfloat16 or wider, within the bound.
No kernel may reach another device: no remote copies, remote signals or barrier semaphores. Data moves between devices by JAX's collectives and lax.ppermute only.
A program may use at most 64 MiB of HBM per device.

v0:
```python
import jax
import jax.numpy as jnp
from jax import lax
from jax.sharding import Mesh
from jax.sharding import PartitionSpec as P

BLK = ("blk_0", "blk_1", "blk_2")
BLK_HEAD = ("blk_0", "blk_1", "blk_2", "head")
norm_epsilon = 1e-06
rope_base = 10000.0
masked_score = -1e30


def joined_along(parts, dim):
    parts = jnp.moveaxis(parts, 0, dim)
    dims = parts.shape
    return parts.reshape(*dims[:dim], dims[dim] * dims[dim + 1], *dims[dim + 2 :])


def from_everyone(value, axis):
    size = lax.axis_size(axis)
    return lax.all_to_all(
        jnp.broadcast_to(value[None], (size, *value.shape)), axis, 0, 0, tiled=True
    )


def collect(value, axis, dim):
    return joined_along(from_everyone(value, axis), dim)


def stacked_from(value, axes, order):
    parts = value[None]
    for k in order:
        parts = lax.all_gather(parts, axes[k], axis=0, tiled=True)
    block = [lax.axis_size(axes[k]) for k in reversed(order)]
    parts = parts.reshape(*block, *value.shape)
    turned = sorted(range(len(order)), key=lambda place: order[len(order) - 1 - place])
    return parts.transpose(*turned, *range(len(order), parts.ndim)).reshape(-1, *value.shape)


def whole_of(value, axes, order, dim):
    return joined_along(stacked_from(value, axes, order), dim)


def lookup(entries, index_array):
    slots = jnp.arange(entries.shape[0], dtype=jnp.int32)
    matches = index_array[..., None] == slots
    return jnp.sum(jnp.where(matches, entries, 0), axis=-1)


def rotate(values, positions):
    half_width = values.shape[-1] // 2
    frequency = rope_base ** (-jnp.arange(half_width, dtype=jnp.float32) / half_width)
    angles = positions.astype(jnp.float32)[..., None] * frequency
    cosine = jnp.cos(angles)
    sine_value = jnp.sin(angles)
    leading = values[..., :half_width]
    trailing = values[..., half_width:]
    return jnp.concatenate(
        [leading * cosine - trailing * sine_value, leading * sine_value + trailing * cosine],
        axis=-1,
    )


def shards(query_nope, query_rope, compressed, latent_gain, key_up, value_up, span_order):
    tokens_here = query_nope.shape[0]
    heads_here = key_up.shape[0]
    nope_width = key_up.shape[1]
    latent_width = key_up.shape[2]
    rope_width = query_rope.shape[1] // heads_here
    value_width = value_up.shape[2]
    half_block = tokens_here // 2
    slice_count = compressed.shape[0]
    block_id = lax.axis_index(BLK)
    head_id = lax.axis_index("head")

    def positions_of(row_ids):
        return lookup(span_order, row_ids // half_block) * half_block + row_ids % half_block

    query_pos = positions_of(block_id * tokens_here + jnp.arange(tokens_here, dtype=jnp.int32))
    own_rows = (
        block_id * tokens_here + head_id * slice_count + jnp.arange(slice_count, dtype=jnp.int32)
    )
    own_pos = positions_of(own_rows)
    latent = compressed[:, :latent_width].astype(jnp.float32)
    latent = (
        latent
        * lax.rsqrt(jnp.mean(latent * latent, axis=1, keepdims=True) + norm_epsilon)
        * latent_gain
    )
    latent = latent.astype(jnp.bfloat16)
    key_rot = rotate(compressed[:, latent_width:].astype(jnp.float32), own_pos).astype(jnp.bfloat16)
    key_rows = jnp.concatenate([latent, key_rot], axis=1)
    nope_parts = query_nope.reshape(tokens_here, heads_here, nope_width)
    query_lat = jnp.einsum(
        "thn,hnl->thl", nope_parts, key_up, preferred_element_type=jnp.float32
    ).astype(jnp.bfloat16)
    query_rot = rotate(
        query_rope.reshape(tokens_here, heads_here, rope_width).astype(jnp.float32),
        query_pos[:, None],
    ).astype(jnp.bfloat16)
    row_count = tokens_here * heads_here
    queries = jnp.concatenate([query_lat, query_rot], axis=2).reshape(
        row_count, latent_width + rope_width
    )
    query_rows_pos = jnp.repeat(query_pos, heads_here)
    score_scale = (nope_width + rope_width) ** (-0.5)
    block_keys = collect(key_rows, "head", 0)
    shard_keys = whole_of(block_keys, BLK, (1, 0, 2), 0)
    row_ids = jnp.arange(shard_keys.shape[0], dtype=jnp.int32)
    run_max = jnp.full((row_count,), masked_score, jnp.float32)
    scores = (
        jnp.einsum("qd,kd->qk", queries, shard_keys, preferred_element_type=jnp.float32)
        * score_scale
    )
    visible = positions_of(row_ids)[None, :] <= query_rows_pos[:, None]
    scores = jnp.where(visible, scores, masked_score)
    new_max = jnp.maximum(run_max, jnp.max(scores, axis=1))
    weight = jnp.where(visible, jnp.exp(scores - new_max[:, None]), 0.0)
    new_sum = jnp.sum(weight, axis=1)
    product = jnp.dot(
        weight.astype(jnp.bfloat16),
        shard_keys[:, :latent_width],
        preferred_element_type=jnp.float32,
    )
    folded = (new_max, new_sum, product)
    run_max, run_sum, run_acc = folded
    lat_out = (
        (run_acc / run_sum[:, None])
        .astype(jnp.bfloat16)
        .reshape(tokens_here, heads_here, latent_width)
    )
    attended = jnp.einsum(
        "thl,hlv->thv", lat_out, value_up, preferred_element_type=jnp.float32
    ).astype(jnp.bfloat16)
    return attended.reshape(tokens_here, heads_here * value_width)


def solution(mesh):
    split = Mesh(
        mesh.devices.reshape(8, 4, 2, mesh.shape["head"]), ("blk_0", "blk_1", "blk_2", "head")
    )
    placed = (
        P(BLK, "head"),
        P(BLK, "head"),
        P(BLK_HEAD, None),
        P(),
        P("head", None, None),
        P("head", None, None),
        P(),
    )
    return jax.shard_map(
        shards, mesh=split, in_specs=placed, out_specs=P(BLK, "head"), check_vma=False
    )
```

profile of v0, /device:TPU:1, one launch (start us, length us, event | category | flops | bytes accessed | tf_op | source)
XLA Modules:
  0.0 131.8 jit_solution(17058499181964433245)
XLA Ops:
  6.5 0.0 copy-start
  6.5 0.0 copy-start.2
  6.5 0.0 all-gather.3.cloned.1.call-start
  6.6 0.9 fusion.34
  7.5 0.7 slice_convert_fusion
  8.2 0.8 select_reduce_fusion.2
  9.0 0.8 fusion.36
  9.8 0.1 fusion.44
  9.9 0.1 pad_maximum_fusion.1
  10.0 11.7 %all_to_all.5 = bf16[8,8,576]{2,1,0:T(8,128)(2,1)S(1)} all-to-all(bf16[8,8,576]{2,1,0:T(8,128)(2,1)S(1)} %broadcast_in_dim.66), channel_id=1, replica_groups=mesh['blk_0'=8,'blk_1'=4,'blk_2'=2,'head'=8] {'head'}, dimensions={0} | all-to-all | bytes 147456 | tf_op jit(solution)/shard_map/all_to_all | solution.py:22
  21.7 18.8 %all_gather.9 = bf16[4,64,576]{2,1,0:T(8,128)(2,1)} all-gather(bf16[1,64,576]{2,1,0:T(8,128)(2,1)S(1)} %bitcast.33), channel_id=1, replica_groups=mesh['blk_0'=8,'blk_1'=4,'blk_2'=2,'head'=8] {'blk_1'}, dimensions={0}, use_global_device_ids=true | all-gather | bytes 368640 | tf_op jit(solution)/shard_map/all_gather | solution.py:34
  40.5 0.0 all-gather.3.cloned.1.call-update
  40.5 0.0 all-gather.5.cloned.1.call-start
  40.6 42.2 %all-gather.3.cloned.1.call-done = bf16[32,64,576]{2,1,0:T(8,128)(2,1)} async-done(((bf16[4,64,576]{2,1,0:T(8,128)(2,1)}), bf16[32,64,576]{2,1,0:T(8,128)(2,1)}) %all-gather.3.cloned.1.call-update) | async-done | bytes 2359312 | tf_op jit(solution)/shard_map/all_gather | solution.py:34
  82.8 0.0 all-gather.5.cloned.1.call-update
  82.8 0.8 select_reduce_fusion.1
  83.7 0.1 broadcast_in_dim.63
  83.8 0.1 le.16
  83.9 1.0 reshape.213
  84.9 0.2 multiply_cosine_fusion
  85.1 0.1 fusion.55
  85.2 0.1 subtract_convert_fusion
  85.3 0.0 copy-done
  85.3 1.2 fusion.11
  86.5 0.1 pad_maximum_fusion
  86.6 0.0 copy-done.2
  86.7 1.3 select_reduce_fusion
  88.0 23.6 %all-gather.5.cloned.1.call-done = bf16[64,64,576]{2,1,0:T(8,128)(2,1)} async-done(((bf16[32,64,576]{2,1,0:T(8,128)(2,1)}), bf16[64,64,576]{2,1,0:T(8,128)(2,1)}) %all-gather.5.cloned.1.call-update) | async-done | bytes 4718608 | tf_op jit(solution)/shard_map/all_gather | solution.py:34
  111.6 3.0 %copy.34 = bf16[8,4,2,64,576]{4,3,2,1,0:T(8,128)(2,1)S(1)} copy(bf16[8,4,2,64,576]{4,3,1,0,2:T(8,128)(2,1)} %bitcast.30) | data formatting | bytes 9437184 | tf_op jit(solution)/shard_map/transpose | solution.py:38
  114.7 4.0 %fusion = (f32[512]{0:T(512)S(1)}, f32[512,4096]{1,0:T(8,128)S(1)}) fusion(s32[4096]{0:T(1024)S(1)} %fusion.37, s32[512]{0:T(512)S(1)} %le.16, bf16[4096,576]{1,0:T(8,128)(2,1)S(1)} %bitcast.31, bf16[64,8,576]{2,0,1:T(8,128)(2,1)S(1)} %pad_maximum_fusion), kind=kOutput, calls=%fused_computation.2 | convolution fusion | flops 2424307200 | bytes 13717504 | tf_op jit(solution)/shard_map/qd,kd->qk/dot_general | solution.py:113
  118.7 2.6 %fusion.1 = f32[512]{0:T(512)S(1)} fusion(f32[512,4096]{1,0:T(8,128)S(1)} %get-tuple-element.16, f32[512]{0:T(512)S(1)} %broadcast_maximum_fusion, s32[4096]{0:T(1024)S(1)} %fusion.37, s32[512]{0:T(512)S(1)} %le.16), kind=kLoop, calls=%fused_computation.3 | loop fusion | flops 12582400 | bytes 8411136 | tf_op jit(solution)/shard_map/reduce_sum | solution.py:120
  121.3 0.0 copy-start.1
  121.3 2.6 %fusion.17 = bf16[64,8,512]{2,1,0:T(8,128)(2,1)S(1)} fusion(bf16[4096,576]{1,0:T(8,128)(2,1)S(1)} %bitcast.32, f32[512,4096]{1,0:T(8,128)S(1)} %get-tuple-element.16, f32[512]{0:T(512)S(1)} %broadcast_maximum_fusion, s32[4096]{0:T(1024)S(1)} %fusion.37, s32[512]{0:T(512)S(1)} %le.16, f32[512]{0:T(512)S(1)} %fusion.1), kind=kOutput, calls=%fused_computation.19 | convolution fusion | flops 2160590848 | bytes 13129728 | tf_op jit(solution)/shard_map/dot_general | solution.py:121
  123.9 0.0 copy-done.1
  123.9 0.4 fusion.12
  124.3 0.7 copy.58
  (10 shorter events, 0.1 us)
Async XLA Ops:
  6.5 78.8 %copy-start = (bf16[8,128,512]{2,1,0:T(8,128)(2,1)S(1)}, bf16[8,128,512]{2,1,0:T(8,128)(2,1)}, u32[]{:S(2)}) copy-start(bf16[8,128,512]{2,1,0:T(8,128)(2,1)} %param.11) | copy-start | bytes 3145732
  6.5 80.1 %copy-start.2 = (s32[128]{0:T(128)S(1)}, s32[128]{0:T(128)}, u32[]{:S(2)}) copy-start(s32[128]{0:T(128)} %param.13) | copy-start | bytes 1540
  6.5 76.3 %all-gather.3.cloned.1.call-start = ((), (), s32[]{:S(2)}) async-start(), calls=%async_computation.1 | async-start | bytes 2949120 | tf_op jit(solution)/shard_map/all_gather | solution.py:34
  40.5 71.1 %all-gather.5.cloned.1.call-start = ((), (), s32[]{:S(2)}) async-start(), calls=%async_computation.2 | async-start | bytes 7864320 | tf_op jit(solution)/shard_map/all_gather | solution.py:34
  121.3 2.6 %copy-start.1 = (bf16[8,512,128]{2,1,0:T(8,128)(2,1)S(1)}, bf16[8,512,128]{2,1,0:T(8,128)(2,1)}, u32[]{:S(2)}) copy-start(bf16[8,512,128]{2,1,0:T(8,128)(2,1)} %param.12) | copy-start | bytes 3145732
Sparse Core Ops, SparseCore 0:
  40.6 42.1 all-gather.2
  84.9 26.6 all-gather.4
where the time goes:
time: 132 us
  waiting for transfers between devices  65.9 us (50%)
  blocking collectives  30.5 us (23%)
  between operations  13.5 us (10%)
  other arithmetic  8.63 us (7%)
  matrix products  8.16 us (6%)
  local copies, waits for them, and re-layouts  5.02 us (4%)
    all_gather x2, waiting for transfers between devices, stacked_from(): parts = lax.all_gather(parts, axes[k], axis=0, tiled=True)  65.9 us
    all_gather x1, blocking collectives, stacked_from(): parts = lax.all_gather(parts, axes[k], axis=0, tiled=True)  18.8 us
    all_to_all x1, blocking collectives, from_everyone(): lax.all_to_all(jnp.broadcast_to(value[None], (size, *value.shape)), axis,...  11.7 us
    dot_general x1, matrix products, shards(): jnp.einsum('qd,kd->qk', queries, shard_keys, preferred_element_type=jnp.f...  4.03 us
    transpose x1, local copies, waits for them, and re-layouts, stacked_from(): parts.transpose(*turned, *range(len(order), parts.ndim))  3.05 us
    reduce_sum x3, other arithmetic, lookup(): return jnp.sum(jnp.where(matches, entries, 0), axis=-1)  2.95 us
  transfers between devices with their start and end apart: 2, of which 2 were waited for; matrix products, arithmetic and copies ran while one was open for 4% of the time, Pallas kernels for 0%

commit v1 on v0

--- a/solution.py
+++ b/solution.py
@@ -31,7 +31,9 @@
 def stacked_from(value, axes, order):
     parts = value[None]
     for k in order:
-        parts = lax.all_gather(parts, axes[k], axis=0, tiled=True)
+        parts = jnp.concatenate(
+            lax.all_to_all(jnp.stack([parts] * lax.axis_size(axes[k])), axes[k], 0, 0), axis=0
+        )
     block = [lax.axis_size(axes[k]) for k in reversed(order)]
     parts = parts.reshape(*block, *value.shape)
     turned = sorted(range(len(order)), key=lambda place: order[len(order) - 1 - place])

time: 132 us -> 127 us (0.962)
  between operations: 13.5 us -> 0.17 us
  blocking collectives: 30.5 us -> 41.6 us
  waiting for transfers between devices: 65.9 us -> 56.1 us
  starting transfers between devices: 0.04 us -> 6.82 us
  other arithmetic: 8.63 us -> 11.3 us
    all_gather x2 -> x0, waiting for transfers between devices: 65.9 us -> none  [stacked_from(): parts = lax.all_gather(parts, axes[k], axis=0, tiled=True)]
    all_to_all x0 -> x1, waiting for transfers between devices: none -> 56.1 us  [stacked_from(): lax.all_to_all(jnp.stack([parts] * lax.axis_size(axes[k])), axes[k], 0, 0)]
    all_to_all x0 -> x2, blocking collectives: none -> 29.9 us  [stacked_from(): lax.all_to_all(jnp.stack([parts] * lax.axis_size(axes[k])), axes[k], 0, 0)]
    all_gather x1 -> x0, blocking collectives: 18.8 us -> none  [stacked_from(): parts = lax.all_gather(parts, axes[k], axis=0, tiled=True)]
    all_to_all x0 -> x1, starting transfers between devices: none -> 6.82 us  [stacked_from(): lax.all_to_all(jnp.stack([parts] * lax.axis_size(axes[k])), axes[k], 0, 0)]
    another operation x2 -> x3, other arithmetic: 0.22 us -> 3.52 us  [the longest x1 3.31 us: stacked_from(): jnp.stack([parts] * lax.axis_size(axes[k]))]
    transpose x1 -> x0, local copies, waits for them, and re-layouts: 3.05 us -> none  [stacked_from(): parts.transpose(*turned, *range(len(order), parts.ndim))]
    another operation x0 -> x3, local copies, waits for them, and re-layouts: none -> 2.57 us  [the longest x2 1.92 us: stacked_from(): jnp.stack([parts] * lax.axis_size(axes[k]))]
  transfers between devices with their start and end apart: 2 -> 1, of which waited for: 2 -> 1; matrix products, arithmetic and copies ran while one was open for 4% -> 2% of each run, Pallas kernels for 0% -> 0%
where the time goes in v1:
time: 127 us
  waiting for transfers between devices  56.1 us (44%)
  blocking collectives  41.6 us (33%)
  other arithmetic  11.3 us (9%)
  matrix products  7.2 us (6%)
  starting transfers between devices  6.82 us (5%)
  local copies, waits for them, and re-layouts  3.7 us (3%)
    all_to_all x1, waiting for transfers between devices, stacked_from(): lax.all_to_all(jnp.stack([parts] * lax.axis_size(axes[k])), axes[k], 0, 0)  56.1 us
    all_to_all x2, blocking collectives, stacked_from(): lax.all_to_all(jnp.stack([parts] * lax.axis_size(axes[k])), axes[k], 0, 0)  29.9 us
    all_to_all x1, blocking collectives, from_everyone(): lax.all_to_all(jnp.broadcast_to(value[None], (size, *value.shape)), axis,...  11.7 us
    all_to_all x1, starting transfers between devices, stacked_from(): lax.all_to_all(jnp.stack([parts] * lax.axis_size(axes[k])), axes[k], 0, 0)  6.82 us
    dot_general x1, matrix products, shards(): jnp.einsum('qd,kd->qk', queries, shard_keys, preferred_element_type=jnp.f...  3.93 us
    another operation x1, other arithmetic, stacked_from(): jnp.stack([parts] * lax.axis_size(axes[k]))  3.31 us
    reduce_sum x1, other arithmetic, shards(): new_sum = jnp.sum(weight, axis=1)  2.62 us
    dot_general x1, matrix products, shards(): jnp.dot(weight.astype(jnp.bfloat16), shard_keys[:, :latent_width], prefer...  2.6 us
  transfers between devices with their start and end apart: 1, of which 1 were waited for; matrix products, arithmetic and copies ran while one was open for 2% of the time, Pallas kernels for 0%

profile of v1, /device:TPU:1, one launch (start us, length us, event | category | flops | bytes accessed | tf_op | source)
XLA Modules:
  0.0 126.8 jit_solution(16265638979630070881)
XLA Ops:
  0.0 0.0 copy-start
  0.0 0.0 copy-start.4
  0.0 0.0 copy-start.3
  0.0 0.0 copy-start.2
  0.0 0.9 fusion.34
  0.9 0.7 slice_convert_fusion
  1.6 0.8 select_reduce_fusion.2
  2.5 0.8 fusion.36
  3.3 0.1 fusion.44
  3.4 0.1 pad_maximum_fusion.2
  3.5 11.7 %all_to_all.20 = bf16[8,8,576]{2,1,0:T(8,128)(2,1)S(1)} all-to-all(bf16[8,8,576]{2,1,0:T(8,128)(2,1)S(1)} %broadcast_in_dim.66), channel_id=1, replica_groups=mesh['blk_0'=8,'blk_1'=4,'blk_2'=2,'head'=8] {'head'}, dimensions={0} | all-to-all | bytes 147456 | tf_op jit(solution)/shard_map/all_to_all | solution.py:22
  15.2 17.6 %all_to_all.21 = bf16[4,1,64,576]{3,2,1,0:T(8,128)(2,1)S(1)} all-to-all(bf16[4,1,64,576]{3,2,1,0:T(8,128)(2,1)S(1)} %stack.9), channel_id=1, replica_groups=mesh['blk_0'=8,'blk_1'=4,'blk_2'=2,'head'=8] {'blk_1'}, dimensions={0} | all-to-all | bytes 589824 | tf_op jit(solution)/shard_map/all_to_all | solution.py:35
  32.8 1.9 %stack.10 = bf16[8,4,64,576]{3,2,1,0:T(8,128)(2,1)} broadcast(bf16[4,64,576]{2,1,0:T(8,128)(2,1)S(1)} %bitcast.35), dimensions={1,2,3} | broadcast | bytes 2654208 | tf_op jit(solution)/shard_map/stack | solution.py:35
  34.7 6.8 %all-to-all-start.2 = ((bf16[8,4,64,576]{3,2,1,0:T(8,128)(2,1)}), bf16[8,4,64,576]{3,2,1,0:T(8,128)(2,1)}, u32[]{:S(2)}, u32[]{:S(2)}) async-start(bf16[8,4,64,576]{3,2,1,0:T(8,128)(2,1)} %stack.10), calls=%async_computation.2 | async-start | bytes 5242880 | tf_op jit(solution)/shard_map/all_to_all | solution.py:35
  41.6 0.0 copy-done.4
  41.6 0.2 select_reduce_fusion.1
  41.8 0.1 broadcast_in_dim.63
  41.8 0.1 le.16
  41.9 0.0 copy-done.3
  42.0 0.1 reshape.215
  42.1 0.2 multiply_cosine_fusion
  42.3 0.1 fusion.55
  42.4 0.1 subtract_convert_fusion
  42.5 0.0 copy-done
  42.5 0.0 copy-done.2
  42.6 0.3 fusion.11
  42.9 0.1 pad_maximum_fusion.1
  43.0 1.3 %select_reduce_fusion = s32[4096]{0:T(1024)S(1)} fusion(s32[128]{0:T(128)S(1)} %copy-done.4, s32[4096]{0:T(1024)S(1)} %add_select_fusion), kind=kLoop, calls=%fused_computation.13 | loop fusion | flops 1568768 | bytes 33280 | tf_op jit(solution)/shard_map/reduce_sum | solution.py:50
  44.3 56.1 %all-to-all-done.2 = bf16[8,4,64,576]{3,2,1,0:T(8,128)(2,1)} async-done(((bf16[8,4,64,576]{3,2,1,0:T(8,128)(2,1)}), bf16[8,4,64,576]{3,2,1,0:T(8,128)(2,1)}, u32[]{:S(2)}, u32[]{:S(2)}) %all-to-all-start.2) | async-done | bytes 2359328 | tf_op jit(solution)/shard_map/all_to_all | solution.py:35
  100.4 3.3 %pad_maximum_fusion = bf16[2,32,64,576]{3,2,1,0:T(8,128)(2,1)S(1)} fusion(bf16[1,32,64,576]{3,2,1,0:T(8,128)(2,1)} %bitcast.4), kind=kLoop, calls=%fused_computation.3 | loop fusion | flops 2359296 | bytes 7077888 | tf_op jit(solution)/shard_map/stack | solution.py:35
  103.7 12.3 %all_to_all.22 = bf16[2,32,64,576]{3,2,1,0:T(8,128)(2,1)S(1)} all-to-all(bf16[2,32,64,576]{3,2,1,0:T(8,128)(2,1)S(1)} %pad_maximum_fusion), channel_id=1, replica_groups=mesh['blk_0'=8,'blk_1'=4,'blk_2'=2,'head'=8] {'blk_2'}, dimensions={0} | all-to-all | bytes 9437184 | tf_op jit(solution)/shard_map/all_to_all | solution.py:35
  115.9 0.7 copy.27
  116.6 3.9 %fusion = (f32[512]{0:T(512)S(1)}, f32[512,4096]{1,0:T(8,128)S(1)}) fusion(s32[4096]{0:T(1024)S(1)} %fusion.37, s32[512]{0:T(512)S(1)} %le.16, bf16[4096,576]{1,0:T(8,128)(2,1)S(1)} %bitcast.33, bf16[64,8,576]{2,0,1:T(8,128)(2,1)S(1)} %pad_maximum_fusion.1), kind=kOutput, calls=%fused_computation.2 | convolution fusion | flops 2424307200 | bytes 13717504 | tf_op jit(solution)/shard_map/qd,kd->qk/dot_general | solution.py:115
  120.5 2.6 %fusion.1 = f32[512]{0:T(512)S(1)} fusion(f32[512,4096]{1,0:T(8,128)S(1)} %get-tuple-element.16, f32[512]{0:T(512)S(1)} %broadcast_maximum_fusion, s32[4096]{0:T(1024)S(1)} %fusion.37, s32[512]{0:T(512)S(1)} %le.16), kind=kLoop, calls=%fused_computation.4 | loop fusion | flops 12582400 | bytes 8411136 | tf_op jit(solution)/shard_map/reduce_sum | solution.py:122
  123.1 0.0 copy-start.1
  123.2 2.6 %fusion.17 = bf16[64,8,512]{2,1,0:T(8,128)(2,1)S(1)} fusion(bf16[4096,576]{1,0:T(8,128)(2,1)S(1)} %bitcast.34, f32[512,4096]{1,0:T(8,128)S(1)} %get-tuple-element.16, f32[512]{0:T(512)S(1)} %broadcast_maximum_fusion, s32[4096]{0:T(1024)S(1)} %fusion.37, s32[512]{0:T(512)S(1)} %le.16, f32[512]{0:T(512)S(1)} %fusion.1), kind=kOutput, calls=%fused_computation.20 | convolution fusion | flops 2160590848 | bytes 13129728 | tf_op jit(solution)/shard_map/dot_general | solution.py:123
  125.8 0.0 copy-done.1
  125.8 0.4 fusion.12
  126.2 0.7 copy.51
  (11 shorter events, 0.1 us)
Async XLA Ops:
  0.0 42.5 %copy-start = (bf16[8,128,512]{2,1,0:T(8,128)(2,1)S(1)}, bf16[8,128,512]{2,1,0:T(8,128)(2,1)}, u32[]{:S(2)}) copy-start(bf16[8,128,512]{2,1,0:T(8,128)(2,1)} %param.11) | copy-start | bytes 3145732
  0.0 41.6 %copy-start.4 = (s32[128]{0:T(128)S(1)}, s32[128]{0:T(128)}, u32[]{:S(2)}) copy-start(s32[128]{0:T(128)} %param.13) | copy-start | bytes 1540
  0.0 41.9 %copy-start.3 = (bf16[64,512]{1,0:T(8,128)(2,1)S(1)}, bf16[64,512]{1,0:T(8,128)(2,1)}, u32[]{:S(2)}) copy-start(bf16[64,512]{1,0:T(8,128)(2,1)} %param.8) | copy-start | bytes 196612
  0.0 42.5 %copy-start.2 = (bf16[64,1024]{1,0:T(8,128)(2,1)S(1)}, bf16[64,1024]{1,0:T(8,128)(2,1)}, u32[]{:S(2)}) copy-start(bf16[64,1024]{1,0:T(8,128)(2,1)} %param.7) | copy-start | bytes 393220
  34.7 65.6 %all-to-all-start.2 = ((bf16[8,4,64,576]{3,2,1,0:T(8,128)(2,1)}), bf16[8,4,64,576]{3,2,1,0:T(8,128)(2,1)}, u32[]{:S(2)}, u32[]{:S(2)}) async-start(bf16[8,4,64,576]{3,2,1,0:T(8,128)(2,1)} %stack.10), calls=%async_computation.2 | async-start | bytes 5242880 | tf_op jit(solution)/shard_map/all_to_all | solution.py:35
  123.1 2.6 %copy-start.1 = (bf16[8,512,128]{2,1,0:T(8,128)(2,1)S(1)}, bf16[8,512,128]{2,1,0:T(8,128)(2,1)}, u32[]{:S(2)}) copy-start(bf16[8,512,128]{2,1,0:T(8,128)(2,1)} %param.12) | copy-start | bytes 3145732
